TPU v7x, 32 devices: a whole 2x2x4 slice. The times are simulated.
32 devices in a mesh: slab: 8 (over z, y), chan: 4 (over x, core).
Axes of the slice: x: 2, y: 2, z: 4, core: 2. Of those that a mesh axis runs over, the one named last changes fastest.
Arguments:
- field: bfloat16 [32, 256, 256, 256], P('chan', 'slab'), may hold values from -6 to 6
- forcing: bfloat16 [256, 256, 256], P('slab', 'chan'), may hold values from -6 to 6
- slot_column: int32 [8, 256], replicated, may hold values from -1 to 1023, as said below
- w_spec: bfloat16 [2, 32, 32, 32768], P(None, 'chan', None, 'slab'), may hold values from -12 to 12
- skip_gain: float32 [32], P('chan'), may hold values from 0.5 to 1.5
- bias: float32 [32], P('chan'), may hold values from -3 to 3
Outputs:
- output: bfloat16 [32, 256, 256, 256], P('chan', 'slab')
- gradient: bfloat16 [32, 256, 256, 256], P('chan', 'slab')
Inputs may be any that keep to these rules, and one draw needn't show every extreme that they name: `slot_column`: every kept pair index 0 to 1023 appears exactly once in the table; empty slots hold -1; the busiest slab device fills all 256 of its slots.
All inputs are finite; a program needn't handle non-finite values.
Results may differ from a plain program's by a relative error of at most 0.022.
Values may be sent and summed in bfloat16 or wider, within the bound.
No kernel may reach another device: no remote copies, remote signals or barrier semaphores. Data moves between devices by JAX's collectives and lax.ppermute only.
A program may use at most 256 MiB of HBM per device.

v0:
```python
import math

import jax
import jax.numpy as jnp
from jax import lax
from jax.sharding import PartitionSpec as P

KXY = 32
KZ = 16


def as_sent(array):
    return jax.tree.map(lambda a: a.astype(jnp.bfloat16) if a.dtype == jnp.float32 else a, array)


def angle_pair(freqs, coords, grid_len):
    turns = freqs[:, None] * coords[None, :] % grid_len
    angle = turns.astype(jnp.float32) * (2.0 * math.pi / grid_len)
    return (jnp.cos(angle), jnp.sin(angle))


def plane_tables(kept, grid_len):
    freqs = jnp.arange(kept, dtype=jnp.int32) - kept // 2
    coords = jnp.arange(grid_len, dtype=jnp.int32)
    cosine, sine = angle_pair(freqs, coords, grid_len)
    row_table = jnp.concatenate([cosine.T, -sine.T], axis=1).astype(jnp.bfloat16)
    col_table = jnp.stack([cosine, sine]).astype(jnp.bfloat16)
    return (row_table, col_table)


def depth_table(kept_z, count, grid_len):
    freqs = jnp.arange(kept_z, dtype=jnp.int32)
    coords = jnp.arange(count, dtype=jnp.int32)
    cosine, sine = angle_pair(freqs, coords, grid_len)
    return jnp.stack([cosine, sine])


def slot_positions(slot_column, columns):
    flat_slots = slot_column.reshape(-1)
    slot_ids = jnp.arange(flat_slots.shape[0], dtype=jnp.int32)
    matches = flat_slots[None, :] == jnp.arange(columns, dtype=jnp.int32)[:, None]
    return jnp.sum(jnp.where(matches, slot_ids[None, :], 0), axis=1)


def gelu_parts(preact):
    coeff = math.sqrt(2.0 / math.pi)
    inner = coeff * (preact + 0.044715 * preact**3)
    tangent = jnp.tanh(inner)
    value = 0.5 * preact * (1.0 + tangent)
    slope = 0.5 * (1.0 + tangent) + 0.5 * preact * (1.0 - tangent * tangent) * coeff * (
        1.0 + 3.0 * 0.044715 * preact * preact
    )
    return (value, slope)


def per_device(field, forcing, slot_column, w_spec, skip_gain, bias):
    channels, z_planes, grid_len, _ = field.shape
    kept = KXY
    kept_z = KZ
    capacity = slot_column.shape[1]
    slabs = lax.axis_size("slab")
    columns = kept * kept
    factor = grid_len ** (-1.5)
    highest = lax.Precision.HIGHEST
    row_table, col_table = plane_tables(kept, grid_len)
    depth_full = depth_table(kept_z, grid_len, grid_len)
    position = slot_positions(slot_column, columns)
    flat_slots = slot_column.reshape(-1)
    occupied = (flat_slots >= 0).astype(jnp.float32)
    clipped = jnp.maximum(flat_slots, 0)
    doubling = jnp.tile(jnp.where(jnp.arange(kept_z) == 0, 1.0, 2.0), capacity).astype(jnp.float32)

    def analyse(volume):
        rows_done = jnp.dot(volume, row_table, preferred_element_type=jnp.float32).astype(
            jnp.bfloat16
        )
        mixed_x = jnp.einsum(
            "tkx,czxj->tkjcz", col_table, rows_done, preferred_element_type=jnp.float32
        )
        real_part = mixed_x[0, :, :kept] + mixed_x[1, :, kept:]
        imag_part = mixed_x[0, :, kept:] - mixed_x[1, :, :kept]
        by_column = jnp.stack([real_part, imag_part], 2).reshape(columns, 2, channels, z_planes)
        packed = jnp.take(by_column, clipped, axis=0) * occupied[:, None, None, None]
        packed = packed.reshape(slabs, capacity, 2, channels, z_planes)
        terms = jnp.einsum(
            "tfz,qrcz->trcqf",
            depth_full,
            lax.all_to_all(
                packed.astype(jnp.bfloat16), "slab", split_axis=0, concat_axis=4, tiled=True
            ).astype(packed.dtype)[0],
            precision=highest,
        )
        owned = jnp.stack([terms[0, 0] + terms[1, 1], terms[0, 1] - terms[1, 0]], 0) * factor
        return owned.reshape(2, channels, capacity * kept_z)

    def synthesise(spectra):
        arranged = spectra.reshape(2, channels, capacity, kept_z).transpose(2, 0, 1, 3)
        terms = jnp.einsum("tfz,qrcf->tqrcz", depth_full, arranged, precision=highest)
        pencils = jnp.stack([terms[0, :, 0] - terms[1, :, 1], terms[1, :, 0] + terms[0, :, 1]], 1)
        returned = lax.all_to_all(
            as_sent(pencils), "slab", split_axis=3, concat_axis=0, tiled=True
        ).astype(pencils.dtype)
        by_column = jnp.take(returned, position, axis=0).astype(jnp.bfloat16)
        by_column = by_column.reshape(kept, kept, 2, channels, z_planes)
        mixed_x = jnp.einsum(
            "tkx,kjrcz->trczxj", col_table, by_column, preferred_element_type=jnp.float32
        )
        joined = jnp.concatenate(
            [mixed_x[0, 0] - mixed_x[1, 1], mixed_x[1, 0] + mixed_x[0, 1]], -1
        ).astype(jnp.bfloat16)
        return jnp.dot(joined, row_table.T, preferred_element_type=jnp.float32) * factor

    plane = lax.all_gather(forcing, "chan", axis=1, tiled=True)
    merged = (field.astype(jnp.float32) + plane.astype(jnp.float32)[None]).astype(jnp.bfloat16)
    coeffs = analyse(merged)
    w_real = w_spec[0].astype(jnp.float32)
    w_imag = w_spec[1].astype(jnp.float32)
    u_real, u_imag = (coeffs[0], coeffs[1])
    out_real = jnp.einsum("com,cm->om", w_real, u_real, precision=highest) - jnp.einsum(
        "com,cm->om", w_imag, u_imag, precision=highest
    )
    out_imag = jnp.einsum("com,cm->om", w_imag, u_real, precision=highest) + jnp.einsum(
        "com,cm->om", w_real, u_imag, precision=highest
    )
    summed = lax.psum_scatter(
        jnp.stack([out_real, out_imag]).astype(jnp.bfloat16),
        "chan",
        scatter_dimension=1,
        tiled=True,
    ).astype(jnp.float32)
    spatial = synthesise(summed * doubling)
    gains = skip_gain[:, None, None, None]
    shifts = bias[:, None, None, None]
    preact = spatial + gains * merged.astype(jnp.float32) + shifts
    value, slope = gelu_parts(preact)
    output = value.astype(jnp.bfloat16)
    grad_pre = output.astype(jnp.float32) * slope
    back_coeffs = analyse(grad_pre.astype(jnp.bfloat16)) * doubling
    all_outputs = lax.all_gather(as_sent(back_coeffs), "chan", axis=1, tiled=True).astype(
        back_coeffs.dtype
    )
    g_real, g_imag = (all_outputs[0], all_outputs[1])
    adj_real = jnp.einsum("com,om->cm", w_real, g_real, precision=highest) + jnp.einsum(
        "com,om->cm", w_imag, g_imag, precision=highest
    )
    adj_imag = jnp.einsum("com,om->cm", w_real, g_imag, precision=highest) - jnp.einsum(
        "com,om->cm", w_imag, g_real, precision=highest
    )
    adjoint_field = synthesise(jnp.stack([adj_real, adj_imag]))
    gradient = (adjoint_field + gains * grad_pre).astype(jnp.bfloat16)
    return (output, gradient)


def solution(mesh):
    placed = (
        P("chan", "slab", None, None),
        P("slab", "chan", None),
        P(),
        P(None, "chan", None, "slab"),
        P("chan"),
        P("chan"),
    )
    return jax.shard_map(
        per_device,
        mesh=mesh,
        in_specs=placed,
        out_specs=(P("chan", "slab", None, None), P("chan", "slab", None, None)),
        check_vma=False,
    )
```

profile of v0, /device:TPU:0, one launch (start us, length us, event | category | flops | bytes accessed | tf_op | source)
XLA Modules:
  0.0 810.1 jit_solution(11574290314864711011)
XLA Ops:
  9.1 37.7 %all-gather.2.cloned.1.call-done = bf16[32,256,256]{2,1,0:T(8,128)(2,1)} async-done(((bf16[32,64,256]{2,1,0:T(8,128)(2,1)}), bf16[32,256,256]{2,1,0:T(8,128)(2,1)}) %all-gather.2.cloned.1.call-update) | async-done | bytes 4194320 | tf_op jit(solution)/shard_map/all_gather | solution.py:113
  53.2 22.3 %fusion.44 = f32[2,32,64,8,32]{2,1,0,4,3:T(8,128)} fusion(bf16[8,32,256,256]{3,2,1,0:T(8,128)(2,1)} %param.10, f32[32,256,256]{2,1,0:T(8,128)} %convert_element_type.136, bf16[1,32,256]{2,1,0:T(8,128)(2,1)S(1)} %get-tuple-element.33, bf16[1,32,256]{2,1,0:T(8,128)(2,1)S(1)} %get-tuple-element.32, bf16[256,32]{0,1:T(8,128)(2,1)S(1)} %get-tuple-element.31, ...), kind=kOutput, calls=%fused_computation.78 | convolution fusion | flops 2739011584 | bytes 46202880 | tf_op jit(solution)/shard_map/tkx,czxj->tkjcz/dot_general | solution.py:77
  75.6 11.6 %slice_add_fusion.3 = (f32[1,32,32,8,32]{2,1,0,4,3:T(8,128)}, f32[1,32,32,8,32]{2,1,0,4,3:T(8,128)}) fusion(f32[2,32,64,8,32]{2,1,0,4,3:T(8,128)} %fusion.44), kind=kLoop, calls=%fused_computation.75 | loop fusion | flops 524288 | bytes 6291456 | tf_op jit(solution)/shard_map/add | solution.py:80
  103.1 21.8 %gather_fusion = f32[2048,2,8,32]{3,2,1,0:T(8,128)} fusion(f32[1024,2,8,32]{3,2,1,0:T(8,128)} %copy.170, s32[2048]{0:T(1024)S(1)} %maximum_clamp_fusion), kind=kCustom, calls=%fused_computation.clone | custom fusion | bytes 8396800 | tf_op jit(solution)/shard_map/jit(_take)/gather | solution.py:83
  124.9 12.3 %fusion.12 = bf16[2048,2,8,32]{3,2,1,0:T(8,128)(2,1)} fusion(f32[2048,2,8,32]{3,2,1,0:T(8,128)} %gather_fusion, f32[2048]{0:T(1024)S(1)} %get-tuple-element.29, pred[2048]{0:T(1024)(128)(4,1)S(1)} %get-tuple-element.28), kind=kLoop, calls=%fused_computation.24 | loop fusion | flops 3145728 | bytes 6301696 | tf_op jit(solution)/shard_map/convert_element_type | solution.py:89
  137.3 9.8 %copy.171 = bf16[8,256,2,8,32]{1,4,3,2,0:T(8,128)(2,1)} copy(bf16[8,256,2,8,32]{4,3,2,1,0:T(8,128)(2,1)} %bitcast.303) | data formatting | bytes 4194304 | tf_op jit(solution)/shard_map/convert_element_type | solution.py:89
  153.1 48.2 %all-to-all-done = bf16[8,256,2,8,32]{1,4,3,2,0:T(8,128)(2,1)S(1)} async-done(((bf16[8,256,2,8,32]{1,4,3,2,0:T(8,128)(2,1)}), bf16[8,256,2,8,32]{1,4,3,2,0:T(8,128)(2,1)S(1)}, u32[]{:S(2)}, u32[]{:S(2)}) %all-to-all-start) | async-done | bytes 2097184 | tf_op jit(solution)/shard_map/all_to_all | solution.py:88
  209.9 19.8 %reduce-scatter.4.cloned.1.call-done = bf16[8,8192]{1,0:T(8,128)(2,1)} async-done(((bf16[32,8192]{1,0:T(8,128)(2,1)}), bf16[8,8192]{1,0:T(8,128)(2,1)}) %reduce-scatter.4.cloned.1.call-update) | async-done | bytes 131088
  249.1 47.3 %all-to-all-done.1 = bf16[256,2,8,256]{0,2,1,3:T(8,128)(2,1)} async-done(((bf16[256,2,8,256]{0,2,1,3:T(8,128)(2,1)}), bf16[256,2,8,256]{0,2,1,3:T(8,128)(2,1)}, u32[]{:S(2)}, u32[]{:S(2)}) %all-to-all-start.1) | async-done | bytes 2097184 | tf_op jit(solution)/shard_map/all_to_all | solution.py:100
  307.1 11.7 %gather_fusion.1 = bf16[1024,2,8,32]{3,2,1,0:T(8,128)(2,1)} fusion(bf16[2048,2,8,32]{3,2,1,0:T(8,128)(2,1)} %bitcast.305, s32[1024]{0:T(1024)S(1)} %fusion.97), kind=kCustom, calls=%fused_computation.1.clone | custom fusion | bytes 2101248 | tf_op jit(solution)/shard_map/jit(_take)/gather | solution.py:103
  327.7 8.9 %copy.239 = bf16[32,32,2,8,32,1]{0,4,5,3,2,1:T(8,128)(2,1)} copy(bf16[32,32,2,8,32,1]{1,0,4,3,2,5:T(8,128)(2,1)} %bitcast.306) | data formatting | bytes 2097152 | tf_op jit(solution)/shard_map/reshape | solution.py:104
  336.7 16.2 %convolution_bitcast_fusion.1 = f32[2,2,8,32,256,32]{4,3,0,2,1,5:T(8,128)} fusion(bf16[32,32,2,8,32,1]{0,4,5,3,2,1:T(8,128)(2,1)} %copy.239, bf16[1,32,256]{2,1,0:T(8,128)(2,1)S(1)} %get-tuple-element.33, bf16[1,32,256]{2,1,0:T(8,128)(2,1)S(1)} %get-tuple-element.32), kind=kOutput, calls=%fused_computation.26 | convolution fusion | flops 536936448 | bytes 34635776 | tf_op jit(solution)/shard_map/tkx,kjrcz->trczxj/dot_general | solution.py:105
  378.1 74.5 %fusion.7 = (f32[8,32,256,256]{3,2,1,0:T(8,128)}, bf16[8,32,256,256]{3,2,1,0:T(8,128)(2,1)}) fusion(f32[8]{0:T(128)S(1)} %copy-done.21, f32[8]{0:T(128)S(1)} %copy-done.16, f32[32,256,256]{2,1,0:T(8,128)} %convert_element_type.136, bf16[8,32,256,256]{3,2,1,0:T(8,128)(2,1)} %param.10, bf16[256,32]{0,1:T(8,128)(2,1)S(1)} %get-tuple-element.31, ...), kind=kOutput, calls=%fused_computation.13 | convolution fusion | flops 2634088448 | bytes 151027776 | tf_op jit(solution)/shard_map/dot_general | solution.py:111
  452.7 29.8 %fusion.47 = f32[2,32,64,8,32]{2,1,0,4,3:T(8,128)} fusion(f32[8,32,256,256]{3,2,1,0:T(8,128)} %get-tuple-element.16, bf16[1,32,256]{2,1,0:T(8,128)(2,1)S(1)} %copy-done.7, bf16[1,32,256]{2,1,0:T(8,128)(2,1)S(1)} %copy-done.5, bf16[256,32]{0,1:T(8,128)(2,1)S(1)} %get-tuple-element.31, bf16[256,32]{0,1:T(8,128)(2,1)S(1)} %get-tuple-element.30), kind=kOutput, calls=%fused_computation.81 | convolution fusion | flops 2705457152 | bytes 71368704 | tf_op jit(solution)/shard_map/tkx,czxj->tkjcz/dot_general | solution.py:77
  482.5 11.5 %slice_add_fusion.2 = (f32[1,32,32,8,32]{2,1,0,4,3:T(8,128)}, f32[1,32,32,8,32]{2,1,0,4,3:T(8,128)}) fusion(f32[2,32,64,8,32]{2,1,0,4,3:T(8,128)} %fusion.47), kind=kLoop, calls=%fused_computation.73 | loop fusion | flops 524288 | bytes 6291456 | tf_op jit(solution)/shard_map/add | solution.py:80
  510.0 21.8 %gather_fusion.2 = f32[2048,2,8,32]{3,2,1,0:T(8,128)} fusion(f32[1024,2,8,32]{3,2,1,0:T(8,128)} %copy.190, s32[2048]{0:T(1024)S(1)} %copy-done.13), kind=kCustom, calls=%fused_computation.2.clone | custom fusion | bytes 8396800 | tf_op jit(solution)/shard_map/jit(_take)/gather | solution.py:83
  531.8 12.4 %fusion.11 = bf16[2048,2,8,32]{3,2,1,0:T(8,128)(2,1)} fusion(f32[2048,2,8,32]{3,2,1,0:T(8,128)} %gather_fusion.2, f32[2048]{0:T(1024)S(1)} %copy-done.11, pred[2048]{0:T(1024)(128)(4,1)S(1)} %copy-done.18), kind=kLoop, calls=%fused_computation.22 | loop fusion | flops 3145728 | bytes 6301696 | tf_op jit(solution)/shard_map/convert_element_type | solution.py:89
  544.2 9.9 %copy.191 = bf16[8,256,2,8,32]{1,4,3,2,0:T(8,128)(2,1)} copy(bf16[8,256,2,8,32]{4,3,2,1,0:T(8,128)(2,1)} %bitcast.302) | data formatting | bytes 4194304 | tf_op jit(solution)/shard_map/convert_element_type | solution.py:89
  557.8 48.4 %all-to-all-done.2 = bf16[8,256,2,8,32]{1,4,3,2,0:T(8,128)(2,1)S(1)} async-done(((bf16[8,256,2,8,32]{1,4,3,2,0:T(8,128)(2,1)}), bf16[8,256,2,8,32]{1,4,3,2,0:T(8,128)(2,1)S(1)}, u32[]{:S(2)}, u32[]{:S(2)}) %all-to-all-start.2) | async-done | bytes 2097184 | tf_op jit(solution)/shard_map/all_to_all | solution.py:88
  632.1 53.0 %all_to_all.48 = bf16[256,2,8,256]{0,2,1,3:T(8,128)(2,1)S(1)} all-to-all(bf16[256,2,8,256]{0,2,1,3:T(8,128)(2,1)} %copy.200), channel_id=1, replica_groups=mesh['slab'=8,'chan'=4] {'slab'}, dimensions={3} | all-to-all | bytes 4194304 | tf_op jit(solution)/shard_map/all_to_all | solution.py:100
  694.3 11.8 %gather_fusion.3 = bf16[1024,2,8,32]{3,2,1,0:T(8,128)(2,1)} fusion(bf16[2048,2,8,32]{3,2,1,0:T(8,128)(2,1)} %bitcast.304, s32[1024]{0:T(1024)S(1)} %copy-done.15), kind=kCustom, calls=%fused_computation.3.clone | custom fusion | bytes 2101248 | tf_op jit(solution)/shard_map/jit(_take)/gather | solution.py:103
  715.0 9.0 %copy.268 = bf16[32,32,2,8,32,1]{0,4,5,3,2,1:T(8,128)(2,1)} copy(bf16[32,32,2,8,32,1]{1,0,4,3,2,5:T(8,128)(2,1)} %bitcast.307) | data formatting | bytes 2097152 | tf_op jit(solution)/shard_map/reshape | solution.py:104
  724.0 16.2 %convolution_bitcast_fusion = f32[2,2,8,32,256,32]{4,3,0,2,1,5:T(8,128)} fusion(bf16[32,32,2,8,32,1]{0,4,5,3,2,1:T(8,128)(2,1)} %copy.268, bf16[1,32,256]{2,1,0:T(8,128)(2,1)S(1)} %copy-done.7, bf16[1,32,256]{2,1,0:T(8,128)(2,1)S(1)} %copy-done.5), kind=kOutput, calls=%fused_computation.25 | convolution fusion | flops 536936448 | bytes 34635776 | tf_op jit(solution)/shard_map/tkx,kjrcz->trczxj/dot_general | solution.py:105
  765.2 37.9 %add_convert_fusion = bf16[8,32,256,256]{3,2,1,0:T(8,128)(2,1)} fusion(f32[8,32,256,256]{3,2,1,0:T(8,128)} %get-tuple-element.16, f32[8]{0:T(128)S(1)} %copy-done.16, bf16[8,32,256,64]{2,1,0,3:T(8,128)(2,1)} %pad_maximum_fusion.1, bf16[256,32]{0,1:T(8,128)(2,1)S(1)} %get-tuple-element.31, bf16[256,32]{0,1:T(8,128)(2,1)S(1)} %get-tuple-element.30), kind=kOutput, calls=%fused_computation.14 | convolution fusion | flops 2214658048 | bytes 109084704 | tf_op jit(solution)/shard_map/dot_general | solution.py:111
  (136 shorter events, 191.5 us)
Async XLA Ops:
  7.2 39.6 %all-gather.2.cloned.1.call-start = ((), (), s32[]{:S(2)}) async-start(), calls=%async_computation.5 | async-start | bytes 5242880 | tf_op jit(solution)/shard_map/all_gather | solution.py:113
  8.6 94.5 %copy-start.12 = (s32[2048]{0:T(1024)}, s32[2048]{0:T(1024)S(1)}, u32[]{:S(2)}) copy-start(s32[2048]{0:T(1024)S(1)} %maximum_clamp_fusion) | copy-start | bytes 24580
  8.6 116.3 %copy-start.10 = (f32[2048]{0:T(1024)}, f32[2048]{0:T(1024)S(1)}, u32[]{:S(2)}) copy-start(f32[2048]{0:T(1024)S(1)} %get-tuple-element.29) | copy-start | bytes 24580
  8.6 116.3 %copy-start.17 = (pred[2048]{0:T(1024)(128)(4,1)}, pred[2048]{0:T(1024)(128)(4,1)S(1)}, u32[]{:S(2)}) copy-start(pred[2048]{0:T(1024)(128)(4,1)S(1)} %get-tuple-element.28) | copy-start | bytes 6148
  8.9 327.8 %copy-start.4 = (bf16[1,32,256]{2,1,0:T(8,128)(2,1)}, bf16[1,32,256]{2,1,0:T(8,128)(2,1)S(1)}, u32[]{:S(2)}) copy-start(bf16[1,32,256]{2,1,0:T(8,128)(2,1)S(1)} %get-tuple-element.32) | copy-start | bytes 49156
  8.9 327.8 %copy-start.6 = (bf16[1,32,256]{2,1,0:T(8,128)(2,1)}, bf16[1,32,256]{2,1,0:T(8,128)(2,1)S(1)}, u32[]{:S(2)}) copy-start(bf16[1,32,256]{2,1,0:T(8,128)(2,1)S(1)} %get-tuple-element.33) | copy-start | bytes 49156
  147.1 54.2 %all-to-all-start = ((bf16[8,256,2,8,32]{1,4,3,2,0:T(8,128)(2,1)}), bf16[8,256,2,8,32]{1,4,3,2,0:T(8,128)(2,1)S(1)}, u32[]{:S(2)}, u32[]{:S(2)}) async-start(bf16[8,256,2,8,32]{1,4,3,2,0:T(8,128)(2,1)} %copy.171), calls=%async_computation | async-start | bytes 4194304 | tf_op jit(solution)/shard_map/all_to_all | solution.py:88
  152.6 77.0 %reduce-scatter.4.cloned.1.call-start = ((), (), s32[]{:S(2)}) async-start(), calls=%async_computation.6 | async-start | bytes 655360
  153.1 78.4 %copy-start = (f32[1,16,256]{2,1,0:T(8,128)}, f32[1,16,256]{2,1,0:T(8,128)S(1)}, u32[]{:S(2)}) copy-start(f32[1,16,256]{2,1,0:T(8,128)S(1)} %get-tuple-element.34) | copy-start | bytes 49156
  153.1 78.4 %copy-start.2 = (f32[1,16,256]{2,1,0:T(8,128)}, f32[1,16,256]{2,1,0:T(8,128)S(1)}, u32[]{:S(2)}) copy-start(f32[1,16,256]{2,1,0:T(8,128)S(1)} %get-tuple-element.35) | copy-start | bytes 49156
  209.8 28.9 %copy-start.8 = (f32[4096]{0:T(1024)}, f32[4096]{0:T(1024)S(1)}, u32[]{:S(2)}) copy-start(f32[4096]{0:T(1024)S(1)} %mul.244) | copy-start | bytes 49156
  242.4 54.0 %all-to-all-start.1 = ((bf16[256,2,8,256]{0,2,1,3:T(8,128)(2,1)}), bf16[256,2,8,256]{0,2,1,3:T(8,128)(2,1)}, u32[]{:S(2)}, u32[]{:S(2)}) async-start(bf16[256,2,8,256]{0,2,1,3:T(8,128)(2,1)} %copy.181), calls=%async_computation.1 | async-start | bytes 4194304 | tf_op jit(solution)/shard_map/all_to_all | solution.py:100
  249.1 74.1 %copy-start.19 = (pred[1024]{0:T(1024)(128)(4,1)}, pred[1024]{0:T(1024)(128)(4,1)S(1)}, u32[]{:S(2)}) copy-start(pred[1024]{0:T(1024)(128)(4,1)S(1)} %compare_and_fusion) | copy-start | bytes 3076
  249.1 69.7 %copy-start.14 = (s32[1024]{0:T(1024)}, s32[1024]{0:T(1024)S(1)}, u32[]{:S(2)}) copy-start(s32[1024]{0:T(1024)S(1)} %fusion.97) | copy-start | bytes 12292
  378.1 74.6 %copy-start.5 = (bf16[1,32,256]{2,1,0:T(8,128)(2,1)S(1)}, bf16[1,32,256]{2,1,0:T(8,128)(2,1)}, u32[]{:S(2)}) copy-start(bf16[1,32,256]{2,1,0:T(8,128)(2,1)} %copy-done.4) | copy-start | bytes 49156
  378.1 74.6 %copy-start.7 = (bf16[1,32,256]{2,1,0:T(8,128)(2,1)S(1)}, bf16[1,32,256]{2,1,0:T(8,128)(2,1)}, u32[]{:S(2)}) copy-start(bf16[1,32,256]{2,1,0:T(8,128)(2,1)} %copy-done.6) | copy-start | bytes 49156
  510.0 21.8 %copy-start.11 = (f32[2048]{0:T(1024)S(1)}, f32[2048]{0:T(1024)}, u32[]{:S(2)}) copy-start(f32[2048]{0:T(1024)} %copy-done.10) | copy-start | bytes 24580
  510.0 21.8 %copy-start.18 = (pred[2048]{0:T(1024)(128)(4,1)S(1)}, pred[2048]{0:T(1024)(128)(4,1)}, u32[]{:S(2)}) copy-start(pred[2048]{0:T(1024)(128)(4,1)} %copy-done.17) | copy-start | bytes 6148
  544.2 13.5 %copy-start.9 = (f32[4096]{0:T(1024)S(1)}, f32[4096]{0:T(1024)}, u32[]{:S(2)}) copy-start(f32[4096]{0:T(1024)} %copy-done.8) | copy-start | bytes 49156
  544.2 62.1 %copy-start.1 = (f32[1,16,256]{2,1,0:T(8,128)S(1)}, f32[1,16,256]{2,1,0:T(8,128)}, u32[]{:S(2)}) copy-start(f32[1,16,256]{2,1,0:T(8,128)} %copy-done) | copy-start | bytes 49156
  544.2 62.1 %copy-start.3 = (f32[1,16,256]{2,1,0:T(8,128)S(1)}, f32[1,16,256]{2,1,0:T(8,128)}, u32[]{:S(2)}) copy-start(f32[1,16,256]{2,1,0:T(8,128)} %copy-done.2) | copy-start | bytes 49156
  554.1 52.1 %all-to-all-start.2 = ((bf16[8,256,2,8,32]{1,4,3,2,0:T(8,128)(2,1)}), bf16[8,256,2,8,32]{1,4,3,2,0:T(8,128)(2,1)S(1)}, u32[]{:S(2)}, u32[]{:S(2)}) async-start(bf16[8,256,2,8,32]{1,4,3,2,0:T(8,128)(2,1)} %copy.191), calls=%async_computation.2 | async-start | bytes 4194304 | tf_op jit(solution)/shard_map/all_to_all | solution.py:88
  685.1 9.1 %copy-start.15 = (s32[1024]{0:T(1024)S(1)}, s32[1024]{0:T(1024)}, u32[]{:S(2)}) copy-start(s32[1024]{0:T(1024)} %copy-done.14) | copy-start | bytes 12292
  694.2 16.2 %copy-start.20 = (pred[1024]{0:T(1024)(128)(4,1)S(1)}, pred[1024]{0:T(1024)(128)(4,1)}, u32[]{:S(2)}) copy-start(pred[1024]{0:T(1024)(128)(4,1)} %copy-done.19) | copy-start | bytes 3076
  (3 other events, 22.9 us)
Sparse Core Ops, SparseCore 0:
  9.6 37.1 all-gather.1
  209.8 19.7 reduce-scatter.3
where the time goes:
time: 821 us; the launch traced here: 810 us
  matrix products  213 us (26%)
  waiting for transfers between devices  202 us (25%)
  local copies, waits for them, and re-layouts  187 us (23%)
  other arithmetic  119 us (14%)
  blocking collectives  59.5 us (7%)
  starting transfers between devices  15.3 us (2%)
  between operations  14.8 us (2%)
    dot_general x2, matrix products, synthesise(): jnp.dot(joined, row_table.T, preferred_element_type=jnp.float32) * factor  112 us
    all_to_all x2, waiting for transfers between devices, analyse(): lax.all_to_all(packed.astype(jnp.bfloat16), 'slab', split_axis=0, concat_...  96.6 us
    all_to_all x1, blocking collectives, synthesise(): lax.all_to_all(as_sent(pencils), 'slab', split_axis=3, concat_axis=0, til...  53 us
    dot_general x2, matrix products, analyse(): jnp.einsum('tkx,czxj->tkjcz', col_table, rows_done, preferred_element_typ...  52.2 us
    all_to_all x1, waiting for transfers between devices, synthesise(): lax.all_to_all(as_sent(pencils), 'slab', split_axis=3, concat_axis=0, til...  47.3 us
    gather x2, local copies, waits for them, and re-layouts, analyse(): jnp.take(by_column, clipped, axis=0) * occupied[:, None, None, None]  43.6 us
    all_gather x1, waiting for transfers between devices, per_device(): plane = lax.all_gather(forcing, 'chan', axis=1, tiled=True)  37.7 us
    dot_general x2, matrix products, synthesise(): jnp.einsum('tkx,kjrcz->trczxj', col_table, by_column, preferred_element_t...  32.4 us
  transfers between devices with their start and end apart: 5, of which 5 were waited for; matrix products, arithmetic and copies ran while one was open for 0% of the time, Pallas kernels for 0%

commit v1 on v0

v1 whole, which is shorter than its diff:
```python
import functools
import math

import jax
import jax.numpy as jnp
import ml_dtypes
import numpy as np
from jax import lax
from jax.experimental import pallas as pl
from jax.experimental.pallas import tpu as pltpu
from jax.sharding import PartitionSpec as P

KXY = 32
KZ = 16
ZB = 4
HALF = ZB * KXY
C1 = math.sqrt(2.0 / math.pi)
C2 = 0.044715
F32 = jnp.float32
BF16 = jnp.bfloat16
SLOTS = 128
VMEM = 56 * 2**20


def dot(a, b):
    return jnp.dot(a, b, preferred_element_type=F32)


def angles(freqs, count, grid_len):
    turns = (freqs[:, None] * np.arange(count)[None, :]) % grid_len
    return turns * (2.0 * math.pi / grid_len)


def half_width(table):
    return table.astype(ml_dtypes.bfloat16)


def plane_tables(grid_len):
    angle = angles(np.arange(KXY) - KXY // 2, grid_len, grid_len)
    cosine, sine = np.cos(angle), np.sin(angle)
    rows = np.zeros((ZB, grid_len, 2, ZB, KXY))
    for i in range(ZB):
        rows[i, :, 0, i, :] = cosine.T
        rows[i, :, 1, i, :] = -sine.T
    rows = rows.reshape(ZB, grid_len, 2 * HALF)
    return rows, np.concatenate([cosine, sine], 0)


def depth_tables(planes, grid_len):
    angle = angles(np.arange(KZ), planes, grid_len)
    cosine, sine = np.cos(angle), np.sin(angle)
    table = np.zeros((planes // ZB, 2, ZB, KXY, 2, KZ, KXY))
    for b in range(planes // ZB):
        for i in range(ZB):
            for j in range(KXY):
                table[b, 0, i, j, 0, :, j] = cosine[:, b * ZB + i]
                table[b, 1, i, j, 0, :, j] = sine[:, b * ZB + i]
                table[b, 0, i, j, 1, :, j] = -sine[:, b * ZB + i]
                table[b, 1, i, j, 1, :, j] = cosine[:, b * ZB + i]
    return table.reshape(planes // ZB, 2 * HALF, 2 * KZ * KXY)


def spread_table():
    return np.repeat(np.eye(SLOTS), KZ, axis=1)


def whole(array):
    return pl.BlockSpec(array.shape, lambda *_: (0,) * len(array.shape))


def scalars():
    return pl.BlockSpec(memory_space=pltpu.SMEM)


def column_sums(u_ref, rt_ref, p_ref, channels):
    total = dot(u_ref[0], rt_ref[0])
    for i in range(1, ZB):
        total += dot(u_ref[i], rt_ref[i])
    total = total.reshape(channels, 2 * KXY, 2 * HALF)
    low, high = total[:, :KXY], total[:, KXY:]
    real = low[:, :, :HALF] + high[:, :, HALF:]
    imag = low[:, :, HALF:] - high[:, :, :HALF]
    p_ref[:, :HALF] = real.reshape(channels * KXY, HALF).astype(BF16)
    p_ref[:, HALF:] = imag.reshape(channels * KXY, HALF).astype(BF16)


def add_depth(p_ref, tz_ref, ph_ref, acc_ref, out_ref, factor):
    step = pl.program_id(0)
    new = dot(p_ref[...], tz_ref[0])

    @pl.when(step == 0)
    def _():
        acc_ref[...] = new

    @pl.when(step > 0)
    def _():
        acc_ref[...] += new

    @pl.when(step == pl.num_programs(0) - 1)
    def _():
        half = KZ * KXY
        cosine, sine = ph_ref[0:1, :], ph_ref[1:2, :]
        real, imag = acc_ref[:, :half], acc_ref[:, half:]
        out_ref[:, :half] = ((real * cosine + imag * sine) * factor).astype(BF16)
        out_ref[:, half:] = ((imag * cosine - real * sine) * factor).astype(BF16)


def turn_spectra(q_ref, ph_ref, turned_ref):
    @pl.when(pl.program_id(0) == 0)
    def _():
        half = KZ * KXY
        cosine, sine = ph_ref[0:1, :], ph_ref[1:2, :]
        real, imag = q_ref[:, :half].astype(F32), q_ref[:, half:].astype(F32)
        turned_ref[:, :half] = (real * cosine - imag * sine).astype(BF16)
        turned_ref[:, half:] = (real * sine + imag * cosine).astype(BF16)


def column_fields(zz_ref, txt, c):
    row = pl.multiple_of(c * KXY, KXY)
    low = zz_ref[pl.ds(row, KXY), :]
    high = jnp.concatenate([-low[:, HALF:], low[:, :HALF]], 1)
    return dot(txt, jnp.concatenate([low, high], 0)).astype(BF16)


def plane_rows(u_ref, tx, c, i, plane):
    row = pl.multiple_of(c * 2 * KXY, 2 * KXY)
    u_ref[i, pl.ds(row, 2 * KXY), :] = dot(tx, plane).astype(BF16)


def analyse_kernel(channels, factor, v_ref, rt_ref, tx_ref, tz_ref, ph_ref, out_ref, acc_ref, p_ref, u_ref):
    tx = tx_ref[...]

    def body(c, carry):
        for i in range(ZB):
            plane_rows(u_ref, tx, c, i, v_ref[c, i])
        return carry

    lax.fori_loop(0, channels, body, 0, unroll=min(channels, 4))
    column_sums(u_ref, rt_ref, p_ref, channels)
    add_depth(p_ref, tz_ref, ph_ref, acc_ref, out_ref, factor)


def analyse(volume, rt, tx, tz, phase, factor):
    channels, planes, rows, grid_len = volume.shape
    width = 2 * KZ * KXY
    return pl.pallas_call(
        functools.partial(analyse_kernel, channels, factor),
        grid=(planes // ZB,),
        in_specs=[
            pl.BlockSpec((channels, ZB, rows, grid_len), lambda b: (0, b, 0, 0)),
            whole(rt),
            whole(tx),
            pl.BlockSpec((1,) + tz.shape[1:], lambda b: (b, 0, 0)),
            whole(phase),
        ],
        out_specs=pl.BlockSpec((channels * KXY, width), lambda b: (0, 0)),
        out_shape=jax.ShapeDtypeStruct((channels * KXY, width), BF16),
        scratch_shapes=[
            pltpu.VMEM((channels * KXY, width), F32),
            pltpu.VMEM((channels * KXY, 2 * HALF), BF16),
            pltpu.VMEM((ZB, channels * 2 * KXY, grid_len), BF16),
        ],
        compiler_params=pltpu.CompilerParams(vmem_limit_bytes=VMEM),
        cost_estimate=pl.CostEstimate(
            flops=512 * volume.size, bytes_accessed=2 * volume.size, transcendentals=0
        ),
        name="analyse",
    )(volume, rt, tx, tz, phase)


def gelu_planes(field, coefs_ref, c):
    cubic, linear, half, square = (coefs_ref[c, k].astype(BF16) for k in range(4))
    squared = field * field
    inner = field * (squared * cubic + linear)
    tangent = jnp.tanh(inner.astype(F32))
    upper = (1.0 + tangent).astype(BF16)
    lower = (1.0 - tangent).astype(BF16)
    value = field * (upper * half)
    slope = upper + value * lower * (squared * square + BF16(2.0 * C1))
    return value, value * slope


def middle_kernel(
    channels, factor, q_ref, v_ref, f_ref, coefs_ref, scale_ref, shift_ref, rt_ref, bd_ref, tx_ref, txt_ref,
    tz_ref, ts_ref, ph_ref, o_ref, g_ref, back_ref, acc_ref, p_ref, u_ref, zz_ref, turned_ref, x_ref,
):
    turn_spectra(q_ref, ph_ref, turned_ref)
    zz_ref[...] = (dot(turned_ref[...], ts_ref[0]) * scale_ref[...] + shift_ref[...]).astype(BF16)
    tx, txt = tx_ref[...], txt_ref[...]

    def columns(c, carry):
        x_ref[c] = column_fields(zz_ref, txt, c)
        return carry

    lax.fori_loop(0, channels, columns, 0, unroll=min(channels, 4))

    def forward(c):
        for i in range(ZB):
            spatial = dot(x_ref[c], bd_ref[i]).astype(BF16)
            value, grad = gelu_planes(spatial + (v_ref[c, i] + f_ref[i]), coefs_ref, c)
            o_ref[c, i] = value
            g_ref[c, i] = grad

    def backward(c):
        for i in range(ZB):
            plane_rows(u_ref, tx, c, i, g_ref[c, i])

    def body(c, carry):
        forward(c)
        backward(c - 1)
        return carry

    forward(0)
    lax.fori_loop(1, channels, body, 0)
    backward(channels - 1)
    column_sums(u_ref, rt_ref, p_ref, channels)
    add_depth(p_ref, tz_ref, ph_ref, acc_ref, back_ref, factor)


def middle(spectra, field, plane, coefs, scale, shift, rt, bd, tx, txt, tz, ts, phase, factor):
    channels, planes, rows, grid_len = field.shape
    width = 2 * KZ * KXY
    volume = pl.BlockSpec((channels, ZB, rows, grid_len), lambda b: (0, b, 0, 0))
    return pl.pallas_call(
        functools.partial(middle_kernel, channels, factor),
        grid=(planes // ZB,),
        in_specs=[
            whole(spectra),
            volume,
            pl.BlockSpec((ZB, rows, grid_len), lambda b: (b, 0, 0)),
            scalars(),
            whole(scale),
            whole(shift),
            whole(rt),
            whole(bd),
            whole(tx),
            whole(txt),
            pl.BlockSpec((1,) + tz.shape[1:], lambda b: (b, 0, 0)),
            pl.BlockSpec((1,) + ts.shape[1:], lambda b: (b, 0, 0)),
            whole(phase),
        ],
        out_specs=[volume, volume, pl.BlockSpec((channels * KXY, width), lambda b: (0, 0))],
        out_shape=[jax.ShapeDtypeStruct(field.shape, BF16)] * 2
        + [jax.ShapeDtypeStruct((channels * KXY, width), BF16)],
        scratch_shapes=[
            pltpu.VMEM((channels * KXY, width), F32),
            pltpu.VMEM((channels * KXY, 2 * HALF), BF16),
            pltpu.VMEM((ZB, channels * 2 * KXY, grid_len), BF16),
            pltpu.VMEM((channels * KXY, 2 * HALF), BF16),
            pltpu.VMEM((channels * KXY, width), BF16),
            pltpu.VMEM((channels, rows, 2 * HALF), BF16),
        ],
        compiler_params=pltpu.CompilerParams(vmem_limit_bytes=VMEM),
        cost_estimate=pl.CostEstimate(
            flops=1024 * field.size, bytes_accessed=6 * field.size, transcendentals=field.size
        ),
        name="middle",
    )(spectra, field, plane, coefs, scale, shift, rt, bd, tx, txt, tz, ts, phase)


def finish_kernel(channels, q_ref, g_ref, gain_ref, bd_ref, txt_ref, ts_ref, ph_ref, o_ref, zz_ref, turned_ref, x_ref):
    turn_spectra(q_ref, ph_ref, turned_ref)
    zz_ref[...] = dot(turned_ref[...], ts_ref[0]).astype(BF16)
    txt = txt_ref[...]

    def columns(c, carry):
        x_ref[c] = column_fields(zz_ref, txt, c)
        return carry

    lax.fori_loop(0, channels, columns, 0, unroll=min(channels, 4))

    def body(c, carry):
        gain = gain_ref[c].astype(F32)
        for i in range(ZB):
            spatial = dot(x_ref[c], bd_ref[i])
            o_ref[c, i] = (spatial + gain * g_ref[c, i].astype(F32)).astype(BF16)
        return carry

    lax.fori_loop(0, channels, body, 0)


def finish(spectra, grads, gain, bd, txt, ts, phase):
    channels, planes, rows, grid_len = grads.shape
    width = 2 * KZ * KXY
    volume = pl.BlockSpec((channels, ZB, rows, grid_len), lambda b: (0, b, 0, 0))
    return pl.pallas_call(
        functools.partial(finish_kernel, channels),
        grid=(planes // ZB,),
        in_specs=[
            whole(spectra),
            volume,
            scalars(),
            whole(bd),
            whole(txt),
            pl.BlockSpec((1,) + ts.shape[1:], lambda b: (b, 0, 0)),
            whole(phase),
        ],
        out_specs=volume,
        out_shape=jax.ShapeDtypeStruct(grads.shape, BF16),
        scratch_shapes=[
            pltpu.VMEM((channels * KXY, 2 * HALF), BF16),
            pltpu.VMEM((channels * KXY, width), BF16),
            pltpu.VMEM((channels, rows, 2 * HALF), BF16),
        ],
        compiler_params=pltpu.CompilerParams(vmem_limit_bytes=VMEM),
        cost_estimate=pl.CostEstimate(
            flops=512 * grads.size, bytes_accessed=4 * grads.size, transcendentals=0
        ),
        name="finish",
    )(spectra, grads, gain, bd, txt, ts, phase)


def depth_mask(lanes):
    depth = lax.broadcasted_iota(jnp.int32, (KZ, 1, lanes), 0)
    lane = lax.broadcasted_iota(jnp.int32, (KZ, 1, lanes), 2)
    return (lane % KZ == depth).astype(F32)


def spread(sums, table, mask, channels):
    out = dot(sums, table)
    out = out.reshape(2, KZ, channels, out.shape[-1]) * mask[None]
    return jnp.sum(out, axis=1)


def gather_depth(values, table_t, mask):
    parts, channels, lanes = values.shape
    out = (values[:, None] * mask[None]).reshape(parts * KZ * channels, lanes)
    return dot(out.astype(BF16), table_t)


LANES = 512


def mix_kernel(groups, s_ref, w_ref, e_ref, o_ref):
    channels, outs, length = w_ref.shape[1:]
    own = outs // groups
    mask = depth_mask(LANES)
    per = SLOTS * KZ // LANES

    def body(k, carry):
        slot = pl.multiple_of(k // per * SLOTS, SLOTS)
        part = pl.multiple_of(k % per * LANES, LANES)
        lane = pl.multiple_of(k * LANES, LANES)
        u = spread(s_ref[:, pl.ds(slot, SLOTS)], e_ref[:, pl.ds(part, LANES)], mask, channels)
        real = jnp.zeros((outs, LANES), F32)
        imag = jnp.zeros((outs, LANES), F32)
        for c in range(channels):
            w0 = w_ref[0, c, :, pl.ds(lane, LANES)].astype(F32)
            w1 = w_ref[1, c, :, pl.ds(lane, LANES)].astype(F32)
            ur, ui = u[0, c : c + 1], u[1, c : c + 1]
            real += w0 * ur - w1 * ui
            imag += w1 * ur + w0 * ui
        for g in range(groups):
            o_ref[g, 0, :, pl.ds(lane, LANES)] = real[g * own : (g + 1) * own].astype(BF16)
            o_ref[g, 1, :, pl.ds(lane, LANES)] = imag[g * own : (g + 1) * own].astype(BF16)
        return carry

    lax.fori_loop(0, length // LANES, body, 0)


def mix(sums, weights, table, groups):
    _, channels, outs, length = weights.shape
    return pl.pallas_call(
        functools.partial(mix_kernel, groups),
        out_shape=jax.ShapeDtypeStruct((groups, 2, outs // groups, length), BF16),
        compiler_params=pltpu.CompilerParams(vmem_limit_bytes=VMEM),
        cost_estimate=pl.CostEstimate(
            flops=4 * weights.size, bytes_accessed=2 * weights.size, transcendentals=0
        ),
        name="mix",
    )(sums, weights, table)


def compress_kernel(p_ref, et_ref, o_ref):
    width = SLOTS * KZ
    mask = depth_mask(width)
    lane = lax.broadcasted_iota(jnp.int32, (1, 1, width), 2)
    twice = jnp.where(lane % KZ == 0, 1.0, 2.0).astype(F32)
    for k in range(p_ref.shape[-1] // width):
        part = p_ref[0, :, :, k * width : (k + 1) * width].astype(F32)
        for g in range(1, p_ref.shape[0]):
            part += p_ref[g, :, :, k * width : (k + 1) * width].astype(F32)
        out = gather_depth(part * twice, et_ref[...], mask)
        o_ref[:, k * SLOTS : (k + 1) * SLOTS] = out.astype(BF16)


def compress(parts, table_t):
    _, _, channels, length = parts.shape
    return pl.pallas_call(
        compress_kernel,
        out_shape=jax.ShapeDtypeStruct((2 * KZ * channels, length // KZ), BF16),
        compiler_params=pltpu.CompilerParams(vmem_limit_bytes=VMEM),
        name="compress",
    )(parts, table_t)


def unmix_kernel(s_ref, w_ref, e_ref, et_ref, o_ref, adj_ref):
    channels, outs, length = w_ref.shape[1:]
    groups = s_ref.shape[0]
    mask = depth_mask(LANES)
    per = SLOTS * KZ // LANES
    wide = depth_mask(SLOTS * KZ)

    def chunk(k, carry):
        def body(j, inner):
            slot = pl.multiple_of(k * SLOTS, SLOTS)
            part = pl.multiple_of(j * LANES, LANES)
            lane = pl.multiple_of(k * SLOTS * KZ + j * LANES, LANES)
            table = e_ref[:, pl.ds(part, LANES)]
            pieces = [spread(s_ref[g, :, pl.ds(slot, SLOTS)], table, mask, outs // groups) for g in range(groups)]
            gr = jnp.concatenate([piece[0] for piece in pieces], 0)
            gi = jnp.concatenate([piece[1] for piece in pieces], 0)
            for c in range(channels):
                w0 = w_ref[0, c, :, pl.ds(lane, LANES)].astype(F32)
                w1 = w_ref[1, c, :, pl.ds(lane, LANES)].astype(F32)
                adj_ref[0, c : c + 1, pl.ds(part, LANES)] = jnp.sum(w0 * gr + w1 * gi, axis=0, keepdims=True)
                adj_ref[1, c : c + 1, pl.ds(part, LANES)] = jnp.sum(w0 * gi - w1 * gr, axis=0, keepdims=True)
            return inner

        lax.fori_loop(0, per, body, 0)
        out = gather_depth(adj_ref[...], et_ref[...], wide)
        o_ref[:, pl.ds(pl.multiple_of(k * SLOTS, SLOTS), SLOTS)] = out.astype(BF16)
        return carry

    lax.fori_loop(0, length // (SLOTS * KZ), chunk, 0)


def unmix(sums, weights, table, table_t):
    _, channels, outs, length = weights.shape
    return pl.pallas_call(
        unmix_kernel,
        out_shape=jax.ShapeDtypeStruct((2 * KZ * channels, length // KZ), BF16),
        scratch_shapes=[pltpu.VMEM((2, channels, SLOTS * KZ), F32)],
        compiler_params=pltpu.CompilerParams(vmem_limit_bytes=VMEM),
        cost_estimate=pl.CostEstimate(
            flops=4 * weights.size, bytes_accessed=2 * weights.size, transcendentals=0
        ),
        name="unmix",
    )(sums, weights, table, table_t)


def per_device(field, forcing, slot_column, w_spec, skip_gain, bias):
    channels, planes, grid_len, _ = field.shape
    slabs, capacity = slot_column.shape
    groups = lax.axis_size("chan")
    own_rows = forcing.shape[1]
    factor = float(grid_len) ** -1.5
    columns = KXY * KXY

    row_np, col_np = plane_tables(grid_len)
    depth_np = depth_tables(planes, grid_len)
    rt = jnp.asarray(half_width(row_np))
    bd = jnp.asarray(half_width(np.swapaxes(row_np, 1, 2)) * ml_dtypes.bfloat16(factor))
    tx = jnp.asarray(half_width(col_np))
    txt = jnp.asarray(half_width(col_np.T))
    tz = jnp.asarray(half_width(depth_np))
    ts = jnp.asarray(half_width(np.swapaxes(depth_np, 1, 2)))
    table = jnp.asarray(half_width(spread_table()))
    table_t = jnp.asarray(half_width(spread_table().T))
    first = np.arange(slabs)[:, None] * planes * np.arange(KZ)[None, :] % grid_len
    first = np.repeat(first * (2.0 * math.pi / grid_len), KXY, axis=1)
    phases = jnp.asarray(np.stack([np.cos(first), np.sin(first)], 1).astype(np.float32))
    phase = lax.dynamic_index_in_dim(phases, lax.axis_index("slab"), 0, keepdims=False)

    numbers = jnp.arange(columns, dtype=jnp.int32)
    to_slots = (numbers[:, None] == slot_column.reshape(1, -1)).astype(BF16)
    to_columns = (slot_column.reshape(-1, 1) == numbers[None, :]).astype(BF16)

    plane = lax.all_gather(forcing, "chan", axis=1, tiled=True)

    def send_sums(coefs):
        by_slot = dot(
            coefs.reshape(channels, KXY, 2 * KZ, KXY).transpose(2, 0, 1, 3).reshape(-1, columns), to_slots
        ).astype(BF16)
        by_slot = by_slot.reshape(-1, slabs, capacity).transpose(1, 0, 2)
        parts = lax.all_to_all(by_slot, "slab", split_axis=0, concat_axis=0, tiled=True)
        return jnp.sum(parts.astype(F32), axis=0)

    def spread_spectra(own):
        everywhere = lax.all_gather(own, "slab", axis=0)
        by_column = jnp.einsum(
            "srk,skn->rn", everywhere, to_columns.reshape(slabs, capacity, columns), preferred_element_type=F32
        ).astype(BF16)
        by_column = by_column.reshape(2 * KZ, channels, KXY, KXY).transpose(1, 2, 0, 3)
        return by_column.reshape(channels * KXY, 2 * KZ * KXY)

    tx_own = lax.dynamic_slice_in_dim(tx, lax.axis_index("chan") * own_rows, own_rows, 1)
    forced = analyse(forcing[None], rt, tx_own, tz, phase, factor)
    forced = lax.psum(forced, "chan").astype(F32)
    coefs = analyse(field, rt, tx, tz, phase, factor).astype(F32)
    coefs = (coefs.reshape(channels, KXY, -1) + forced[None]).astype(BF16)
    sums = send_sums(coefs).astype(BF16)
    partial = mix(sums, w_spec, table, groups)
    parts = lax.all_to_all(partial, "chan", split_axis=0, concat_axis=0, tiled=True)
    spectra = spread_spectra(compress(parts, table_t))

    gain_rows = jnp.repeat(skip_gain, KXY)[:, None]
    centre = np.zeros((KXY, 2, ZB, KXY), np.float32)
    centre[KXY // 2, 0, :, KXY // 2] = 1.0 / factor
    centre = jnp.asarray(np.tile(centre.reshape(KXY, 2 * HALF), (channels, 1)))
    shift = centre * jnp.repeat(bias / skip_gain, KXY)[:, None]
    coefs_gelu = jnp.stack(
        [skip_gain**3 * (C1 * C2), skip_gain * C1, skip_gain * 0.5, skip_gain**2 * (6.0 * C1 * C2)], 1
    )
    output, grads, back = middle(
        spectra, field, plane, coefs_gelu, 1.0 / gain_rows, shift, rt, bd, tx, txt, tz, ts, phase, 0.5 * factor
    )
    doubling = jnp.where(jnp.arange(KZ) == 0, 1.0, 2.0).astype(F32)
    doubling = jnp.tile(jnp.repeat(doubling, channels), 2)[:, None]
    sums = (send_sums(back) * doubling).astype(BF16)
    everyone = lax.all_gather(sums, "chan", axis=0)
    adjoint = spread_spectra(unmix(everyone, w_spec, table, table_t))
    gradient = finish(adjoint, grads, skip_gain * 0.5, bd, txt, ts, phase)
    return output, gradient


def solution(mesh):
    placed = (
        P("chan", "slab", None, None),
        P("slab", "chan", None),
        P(),
        P(None, "chan", None, "slab"),
        P("chan"),
        P("chan"),
    )
    return jax.shard_map(
        per_device,
        mesh=mesh,
        in_specs=placed,
        out_specs=(P("chan", "slab", None, None), P("chan", "slab", None, None)),
        check_vma=False,
    )
```

time: 821 us -> 419 us (0.51); the launches traced: 810 us -> 418 us
  matrix products: 213 us -> 9.73 us
  Pallas kernels: 0 us -> 157 us
  local copies, waits for them, and re-layouts: 187 us -> 39.9 us
  other arithmetic: 119 us -> 7.81 us
  waiting for transfers between devices: 202 us -> 134 us
  blocking collectives: 59.5 us -> 49.9 us
  starting transfers between devices: 15.3 us -> 5.89 us
    dot_general x10 -> x4, matrix products: 213 us -> 9.73 us  [the longest x2 6.08 us: spread_spectra(): jnp.einsum('srk,skn->rn', everywhere, to_columns.reshape(slabs, capacity,...]
    pallas_call x0 -> x7, Pallas kernels: none -> 157 us  [the longest x1 76.9 us: middle(): pl.pallas_call(functools.partial(middle_kernel, channels, factor), grid=(...]
    all_to_all x3 -> x1, waiting for transfers between devices: 144 us -> 25.7 us  [send_sums(): lax.all_to_all(by_slot, 'slab', split_axis=0, concat_axis=0, tiled=True)]
    gather x6 -> x0, local copies, waits for them, and re-layouts: 75.9 us -> none  [the longest x2 43.6 us: analyse(): jnp.take(by_column, clipped, axis=0) * occupied[:, None, None, None]]
    all_gather x0 -> x2, waiting for transfers between devices: none -> 73.3 us  [spread_spectra(): everywhere = lax.all_gather(own, 'slab', axis=0)]
    add x9 -> x0, other arithmetic: 41.2 us -> none  [the longest x2 23.1 us: analyse(): real_part = mixed_x[0, :, :kept] + mixed_x[1, :, kept:]]
    convert_element_type x4 -> x0, local copies, waits for them, and re-layouts: 36.5 us -> none  [the longest x2 19.7 us: analyse(): packed.astype(jnp.bfloat16)]
    convert_element_type x6 -> x1, other arithmetic: 31.7 us -> 0.1 us  [per_device(): sums = (send_sums(back) * doubling).astype(BF16)]
  transfers between devices with their start and end apart: 5 -> 5, of which waited for: 5 -> 5; matrix products, arithmetic and copies ran while one was open for 0% -> 5% of each run, Pallas kernels for 0% -> 5%
where the time goes in v1:
time: 419 us; the launch traced here: 418 us
  Pallas kernels  157 us (37%)
  waiting for transfers between devices  134 us (32%)
  blocking collectives  49.9 us (12%)
  local copies, waits for them, and re-layouts  39.9 us (10%)
  between operations  13.9 us (3%)
  matrix products  9.73 us (2%)
  other arithmetic  7.81 us (2%)
  starting transfers between devices  5.89 us (1%)
    pallas_call x1, Pallas kernels, middle(): pl.pallas_call(functools.partial(middle_kernel, channels, factor), grid=(...  76.9 us
    all_gather x2, waiting for transfers between devices, spread_spectra(): everywhere = lax.all_gather(own, 'slab', axis=0)  73.3 us
    pallas_call x1, Pallas kernels, finish(): pl.pallas_call(functools.partial(finish_kernel, channels), grid=(planes /...  33.1 us
    all_to_all x1, blocking collectives, send_sums(): lax.all_to_all(by_slot, 'slab', split_axis=0, concat_axis=0, tiled=True)  30 us
    pallas_call x2, Pallas kernels, analyse(): pl.pallas_call(functools.partial(analyse_kernel, channels, factor), grid=...  28.6 us
    all_to_all x1, waiting for transfers between devices, send_sums(): lax.all_to_all(by_slot, 'slab', split_axis=0, concat_axis=0, tiled=True)  25.7 us
    all_gather x1, waiting for transfers between devices, per_device(): plane = lax.all_gather(forcing, 'chan', axis=1, tiled=True)  23.1 us
    all_to_all x1, blocking collectives, per_device(): lax.all_to_all(partial, 'chan', split_axis=0, concat_axis=0, tiled=True)  13 us
  transfers between devices with their start and end apart: 5, of which 5 were waited for; matrix products, arithmetic and copies ran while one was open for 5% of the time, Pallas kernels for 5%

profile of v1, /device:TPU:0, one launch (start us, length us, event | category | flops | bytes accessed | tf_op | source)
XLA Modules:
  0.0 418.2 jit_solution(17334987840081038368)
XLA Ops:
  9.9 8.4 %analyse.3 = bf16[32,1024]{1,0:T(8,128)(2,1)} custom-call(bf16[1,32,64,256]{3,2,1,0:T(8,128)(2,1)} %bitcast.69, bf16[4,256,256]{2,1,0:T(8,128)(2,1)} %constant.58.clone.rt_ref, bf16[64,64]{1,0:T(8,128)(2,1)} %constant_dynamic-slice_fusion.tx_ref, bf16[8,256,1024]{2,1,0:T(8,128)(2,1)} %constant.62.clone.tz_ref, f32[2,512]{1,0:T(2,128)} %dynamic-slice_bitcast_fusion.ph_ref), custom_call_target="tpu_custom_call" | custom-call | flops 268435456 | bytes 1048576 | tf_op jit(solution)/shard_map/analyse/pallas_call | solution.py:146
  20.2 20.2 %analyse.2 = bf16[256,1024]{1,0:T(8,128)(2,1)} custom-call(bf16[8,32,256,256]{3,2,1,0:T(8,128)(2,1)} %v_ref.3, bf16[4,256,256]{2,1,0:T(8,128)(2,1)} %constant.58.clone.rt_ref, bf16[64,256]{1,0:T(8,128)(2,1)} %constant.60.clone.tx_ref, bf16[8,256,1024]{2,1,0:T(8,128)(2,1)} %constant.62.clone.tz_ref, f32[2,512]{1,0:T(2,128)} %dynamic-slice_bitcast_fusion.ph_ref), custom_call_target="tpu_custom_call" | custom-call | flops 8589934592 | bytes 33554432 | tf_op jit(solution)/shard_map/analyse/pallas_call | solution.py:146
  40.4 3.9 reshape.124
  44.3 10.7 %all-reduce.2.cloned.1.call-done = bf16[32,32,32]{2,1,0:T(8,128)(2,1)} async-done(((bf16[32,32,32]{2,1,0:T(8,128)(2,1)}), bf16[32,32,32]{2,1,0:T(8,128)(2,1)}) %all-reduce.2.cloned.1.call-update) | async-done | bytes 65552 | tf_op jit(solution)/shard_map/psum | solution.py:489
  56.0 4.7 %fusion.11 = bf16[32,8,32,32]{3,2,1,0:T(8,128)(2,1)S(1)} fusion(f32[8,32,32,32]{3,2,1,0:T(8,128)} %reshape.124, f32[32,32,32]{2,0,1:T(8,128)S(1)} %copy.34), kind=kLoop, calls=%fused_computation.14 | loop fusion | flops 524288 | bytes 1703936 | tf_op jit(solution)/shard_map/transpose | solution.py:473
  64.8 30.0 %all_to_all.15 = bf16[8,256,256]{2,1,0:T(8,128)(2,1)S(1)} all-to-all(bf16[8,256,256]{2,1,0:T(8,128)(2,1)S(1)} %bitcast.70), channel_id=1, replica_groups=mesh['slab'=8,'chan'=4] {'slab'}, dimensions={0} | all-to-all | bytes 2097152 | tf_op jit(solution)/shard_map/all_to_all | solution.py:476
  95.6 6.8 %mix.1 = bf16[4,2,8,4096]{3,2,1,0:T(8,128)(2,1)} custom-call(bf16[256,256]{1,0:T(8,128)(2,1)} %reduce_sum.23.s_ref, bf16[2,8,32,4096]{3,2,1,0:T(8,128)(2,1)} %w_ref.3, bf16[128,2048]{1,0:T(8,128)(2,1)} %constant.64.clone.e_ref), custom_call_target="tpu_custom_call" | custom-call | flops 8388608 | bytes 4194304 | tf_op jit(solution)/shard_map/mix/pallas_call | solution.py:363
  102.5 13.0 %all_to_all.16.p_ref = bf16[4,2,8,4096]{3,2,1,0:T(8,128)(2,1)} all-to-all(bf16[4,2,8,4096]{3,2,1,0:T(8,128)(2,1)} %mix.1), channel_id=1, replica_groups=mesh['slab'=8,'chan'=4] {'chan'}, dimensions={0} | all-to-all | bytes 1048576 | tf_op jit(solution)/shard_map/all_to_all | solution.py:494
  122.2 34.3 %all-gather.8.cloned.1.call-done = bf16[2048,256]{1,0:T(8,128)(2,1)} async-done(((bf16[256,256]{1,0:T(8,128)(2,1)}), bf16[2048,256]{1,0:T(8,128)(2,1)}) %all-gather.8.cloned.1.call-update) | async-done | bytes 1048592 | tf_op jit(solution)/shard_map/all_gather | solution.py:480
  156.5 3.0 fusion.15
  161.3 2.7 copy.61
  164.0 4.3 %reshape.117.q_ref = bf16[256,1024]{1,0:T(8,128)(2,1)} reshape(bf16[8,32,32,32]{3,2,1,0:T(8,128)(2,1)} %bitcast.66) | data formatting | bytes 1048576 | tf_op jit(solution)/shard_map/reshape | solution.py:485
  168.3 23.1 %all-gather.6.cloned.1.call-done.f_ref = bf16[32,256,256]{2,1,0:T(8,128)(2,1)} async-done(((bf16[32,64,256]{2,1,0:T(8,128)(2,1)}), bf16[32,256,256]{2,1,0:T(8,128)(2,1)}) %all-gather.6.cloned.1.call-update) | async-done | bytes 4194320 | tf_op jit(solution)/shard_map/all_gather | solution.py:469
  191.4 76.9 %middle.1 = (bf16[8,32,256,256]{3,2,1,0:T(8,128)(2,1)}, bf16[8,32,256,256]{3,2,1,0:T(8,128)(2,1)}, bf16[256,1024]{1,0:T(8,128)(2,1)}) custom-call(bf16[256,1024]{1,0:T(8,128)(2,1)} %reshape.117.q_ref, bf16[8,32,256,256]{3,2,1,0:T(8,128)(2,1)} %v_ref.3, bf16[32,256,256]{2,1,0:T(8,128)(2,1)} %all-gather.6.cloned.1.call-done.f_ref, ...), custom_call_target="tpu_custom_call" | custom-call | flops 17179869184 | bytes 100663296 | tf_op jit(solution)/shard_map/middle/pallas_call | solution.py:224
  268.3 2.9 reshape.118
  273.3 3.5 reshape.119
  279.7 5.5 %all-to-all-start.2 = ((bf16[8,256,256]{2,1,0:T(8,128)(2,1)}), bf16[8,256,256]{2,1,0:T(8,128)(2,1)S(1)}, u32[]{:S(2)}, u32[]{:S(2)}) async-start(bf16[8,256,256]{2,1,0:T(8,128)(2,1)} %bitcast.63), calls=%async_computation.2 | async-start | bytes 2097152 | tf_op jit(solution)/shard_map/all_to_all | solution.py:476
  285.6 25.7 %all-to-all-done.2 = bf16[8,256,256]{2,1,0:T(8,128)(2,1)S(1)} async-done(((bf16[8,256,256]{2,1,0:T(8,128)(2,1)}), bf16[8,256,256]{2,1,0:T(8,128)(2,1)S(1)}, u32[]{:S(2)}, u32[]{:S(2)}) %all-to-all-start.2) | async-done | bytes 1048608 | tf_op jit(solution)/shard_map/all_to_all | solution.py:476
  311.6 7.0 %all_gather.22.s_ref = bf16[4,256,256]{2,1,0:T(8,128)(2,1)} all-gather(bf16[1,256,256]{2,1,0:T(8,128)(2,1)S(1)} %fusion.16), channel_id=1, replica_groups=mesh['slab'=8,'chan'=4] {'chan'}, dimensions={0}, use_global_device_ids=true | all-gather | bytes 655360 | tf_op jit(solution)/shard_map/all_gather | solution.py:511
  318.6 9.3 %unmix.1 = bf16[256,256]{1,0:T(8,128)(2,1)} custom-call(bf16[4,256,256]{2,1,0:T(8,128)(2,1)} %all_gather.22.s_ref, bf16[2,8,32,4096]{3,2,1,0:T(8,128)(2,1)} %w_ref.3, bf16[128,2048]{1,0:T(8,128)(2,1)} %constant.64.clone.e_ref, bf16[2048,128]{1,0:T(8,128)(2,1)} %constant.65.clone.et_ref), custom_call_target="tpu_custom_call" | custom-call | flops 8388608 | bytes 4194304 | tf_op jit(solution)/shard_map/unmix/pallas_call | solution.py:430
  327.9 39.1 %all-gather.10.cloned.1.call-done = bf16[2048,256]{1,0:T(8,128)(2,1)} async-done(((bf16[256,256]{1,0:T(8,128)(2,1)}), bf16[2048,256]{1,0:T(8,128)(2,1)}) %all-gather.10.cloned.1.call-update) | async-done | bytes 1048592 | tf_op jit(solution)/shard_map/all_gather | solution.py:480
  367.0 3.0 fusion.14
  374.3 4.2 %reshape.122.q_ref = bf16[256,1024]{1,0:T(8,128)(2,1)} reshape(bf16[8,32,32,32]{3,2,1,0:T(8,128)(2,1)} %bitcast.68) | data formatting | bytes 1048576 | tf_op jit(solution)/shard_map/reshape | solution.py:485
  378.5 33.1 %finish.1 = bf16[8,32,256,256]{3,2,1,0:T(8,128)(2,1)} custom-call(bf16[256,1024]{1,0:T(8,128)(2,1)} %reshape.122.q_ref, bf16[8,32,256,256]{3,2,1,0:T(8,128)(2,1)} %get-tuple-element.7.g_ref, f32[8]{0:T(128)} %get-tuple-element.8.gain_ref, bf16[4,256,256]{2,1,0:T(8,128)(2,1)} %constant.59.clone.bd_ref, bf16[256,64]{1,0:T(8,128)(2,1)} %constant.61.clone.txt_ref, ...), custom_call_target="tpu_custom_call" | custom-call | flops 8589934592 | bytes 67108864 | tf_op jit(solution)/shard_map/finish/pallas_call | solution.py:286
  (49 shorter events, 28.9 us)
Async XLA Ops:
  7.2 47.8 %all-reduce.2.cloned.1.call-start = ((), (), s32[]{:S(2)}) async-start(), calls=%async_computation.3 | async-start | bytes 524288 | tf_op jit(solution)/shard_map/psum | solution.py:489
  20.1 20.3 %copy-start.1 = (s32[8,256]{1,0:T(8,128)S(1)}, s32[8,256]{1,0:T(8,128)}, u32[]{:S(2)}) copy-start(s32[8,256]{1,0:T(8,128)} %param.18) | copy-start | bytes 24580
  20.1 136.4 %all-gather.8.cloned.1.call-start = ((), (), s32[]{:S(2)}) async-start(), calls=%async_computation.5 | async-start | bytes 1179648 | tf_op jit(solution)/shard_map/all_gather | solution.py:480
  95.6 23.3 %copy-start.2 = (f32[8]{0:T(128)S(1)}, f32[8]{0:T(128)}, u32[]{:S(2)}) copy-start(f32[8]{0:T(128)} %param.20) | copy-start | bytes 100
  95.6 23.3 %copy-start.3 = (f32[8]{0:T(128)S(1)}, f32[8]{0:T(128)}, u32[]{:S(2)}) copy-start(f32[8]{0:T(128)} %param.21) | copy-start | bytes 100
  95.6 25.8 %copy-start = (f32[256,256]{1,0:T(8,128)S(1)}, f32[256,256]{1,0:T(8,128)}, u32[]{:S(2)}) copy-start(f32[256,256]{1,0:T(8,128)} %constant.67.clone) | copy-start | bytes 786436
  118.1 73.3 %all-gather.6.cloned.1.call-start = ((), (), s32[]{:S(2)}) async-start(), calls=%async_computation.4 | async-start | bytes 5242880 | tf_op jit(solution)/shard_map/all_gather | solution.py:469
  279.7 31.7 %all-to-all-start.2 = ((bf16[8,256,256]{2,1,0:T(8,128)(2,1)}), bf16[8,256,256]{2,1,0:T(8,128)(2,1)S(1)}, u32[]{:S(2)}, u32[]{:S(2)}) async-start(bf16[8,256,256]{2,1,0:T(8,128)(2,1)} %bitcast.63), calls=%async_computation.2 | async-start | bytes 2097152 | tf_op jit(solution)/shard_map/all_to_all | solution.py:476
  285.2 81.8 %all-gather.10.cloned.1.call-start = ((), (), s32[]{:S(2)}) async-start(), calls=%async_computation.6 | async-start | bytes 1179648 | tf_op jit(solution)/shard_map/all_gather | solution.py:480
Sparse Core Ops, SparseCore 0:
  20.2 34.6 all-reduce.1
  118.2 38.2 all-gather.7
  158.1 33.2 all-gather.5
  328.1 38.9 all-gather.9
